TPU v7x, 32 devices: a whole 2x2x4 slice. The times are simulated.
32 devices in a mesh: gx: 8 (over y, x, core), gy: 4 (over z).
Axes of the slice: x: 2, y: 2, z: 4, core: 2. Of those that a mesh axis runs over, the one named last changes fastest.
Arguments:
- thermal_anomaly: float32 [32, 12, 38400], P(('gx', 'gy')), may hold values from -4 to 4
- zonal_flow_ratio: float32 [32, 12, 38400], P(('gx', 'gy')), may hold values from -0.9 to 0.9
- meridional_flow_ratio: float32 [32, 12, 38400], P(('gx', 'gy')), may hold values from -0.9 to 0.9
- diffusion_rates: float32 [32, 11, 38400], P(('gx', 'gy')), may hold values from 0.05 to 5
- ocean_bottom_scaled: float32 [32, 38400], P(('gx', 'gy')), may hold values from 0.5 to 2
- ocean_indicator: int32 [32, 38400], P(('gx', 'gy')), may hold values 0 or 1
- operator_diagonal: float32 [32, 38400], P(('gx', 'gy')), may hold values from 0.05 to 0.5
- elevation_source: float32 [32, 38400], P(('gx', 'gy')), may hold values from -32 to 32
- block_positions: int32 [32], replicated, may hold values from 0 to 31, as said below
Outputs:
- new_temp: float32 [32, 12, 38400], P(('gx', 'gy'))
- surface_height: float32 [32, 38400], P(('gx', 'gy'))
Inputs may be any that keep to these rules, and one draw needn't show every extreme that they name: `block_positions`: A permutation of 0 to 31. Tiles held by consecutive devices (the last and the first counted as consecutive) share an edge of the tile grid, which is periodic along x, except for two such pairs, 16 apart.
All inputs are finite; a program needn't handle non-finite values. No bound on the sum of `ocean_indicator` on one device may be relied on, other than what follows from the above.
Results may differ from a plain program's by a relative error of at most 0.0001.
Values sent between devices are 32-bit elements; how exact they have to be, the bound alone decides.
No kernel may reach another device: no remote copies, remote signals or barrier semaphores. Data moves between devices by JAX's collectives and lax.ppermute only.
A program may use at most 128 MiB of HBM per device.

v0:
```python
import functools

import jax
import jax.numpy as jnp
from jax import lax
from jax.experimental import pallas as pl
from jax.experimental.pallas import tpu as pltpu
from jax.sharding import PartitionSpec as P

ITERS = 4
SPAN_X = 240
SPAN_Y = 160
RIM = 4
ADVECT = 0.25
DIFFUSE = 0.12
STERIC = 0.5
LOW_RATE = 0.05
HIGH_RATE = 32.5
ROOTS = (0.02, 0.35, 0.1, 0.2)
STRETCH = 4.0
TINY = 1e-30
BOTH = ("gx", "gy")
SIDES = ((-1, 0), (1, 0), (0, -1), (0, 1), (-1, -1), (1, -1), (-1, 1), (1, 1))

LANES = 128
GROUP = 8
GROUPS = SPAN_Y // GROUP
PLANES = GROUP * SPAN_X // LANES
ROWS = GROUPS * PLANES
SLABS = GROUPS + 4
WIDE = SLABS * PLANES
START = [SPAN_X * j // LANES for j in range(GROUP)]
OFF = [SPAN_X * j % LANES for j in range(GROUP)]
LAST = [(SPAN_X * j + SPAN_X - 1) // LANES for j in range(GROUP)]
END = [(SPAN_X * j + SPAN_X - 1) % LANES for j in range(GROUP)]
FIRST_OF = [[OFF[j] for j in range(GROUP) if START[j] == a] for a in range(PLANES)]
LAST_OF = [[END[j] for j in range(GROUP) if LAST[j] == a] for a in range(PLANES)]
RIM_ROWS = 20
HELD = -(-ROWS // 8) * 8
PACKS = 3 * HELD
FIELDS = PACKS + 56
EDGE = 32
BUDGET = 32 * 1024 * 1024


def turn(value, shift, axis=1):
    shift = shift % value.shape[axis]
    return value if shift == 0 else pltpu.roll(value, shift, axis)


def fetching(pairs, sems):
    copies = [pltpu.make_async_copy(a, b, sems.at[n]) for n, (a, b) in enumerate(pairs)]
    for copy in copies:
        copy.start()
    return copies


def pieces_of(levels, count):
    rows = 2 * levels
    number = -(-4 * rows // count)
    runs = [[] for _ in range(4)]
    for c in range(4):
        for j in range(number):
            low, high = max(c * rows, j * count), min((c + 1) * rows, (j + 1) * count)
            if low < high:
                runs[c].append((j, low - j * count, low - c * rows, high - low))
    return number, runs


class Level:
    def __init__(self, ref, base):
        self.ref, self.base = ref, base

    def plane(self, a):
        return self.ref[comb(self.base + a), :]

    def rows(self, low, size):
        return self.ref[pl.ds(self.base + low, size), :]


def lane_of(shape):
    return lax.broadcasted_iota(jnp.int32, shape, len(shape) - 1)


def row_of(shape):
    return lax.broadcasted_iota(jnp.int32, shape, 0)


def comb(a, count=GROUPS):
    return pl.ds(a, count, stride=PLANES)


def line_of(get, y):
    lane = lane_of((1, LANES))
    j = y % GROUP
    row = y // GROUP * PLANES + START[j]
    first, second = get(row), get(row + 1)
    third = get(row + 2) if START[j] + 2 < PLANES else second
    left = turn(jnp.where(lane >= OFF[j], first, second), -OFF[j])
    right = turn(jnp.where(lane >= OFF[j], second, third), -OFF[j])
    return left, right


def drop(value, lanes, lane):
    for at in lanes:
        value = jnp.where(lane == at, 0.0, value)
    return value


def store_terms(a, temp, flow_x, flow_y, te, tw, tn, ts):
    spread = DIFFUSE * temp
    te[a] = spread - flow_x
    tw[a] = spread + flow_x
    tn[a, 8 : 8 + GROUPS] = spread - flow_y
    ts[a, 8 : 8 + GROUPS] = spread + flow_y


def clear_terms(tn, ts):
    none = jnp.zeros((PLANES, 1, LANES), jnp.float32)
    for ref in (tn, ts):
        ref[:, 7:8] = none
        ref[:, 8 + GROUPS : 9 + GROUPS] = none


def inner_sum(a, te, tw, tn, ts):
    lane = lane_of((GROUPS, LANES))
    here = te[a]
    east = here if a == PLANES - 1 else jnp.where(lane == 0, te[a + 1], here)
    east = drop(turn(east, -1), LAST_OF[a], lane)
    here = tw[a]
    west = here if a == 0 else jnp.where(lane == LANES - 1, tw[a - 1], here)
    west = drop(turn(west, 1), FIRST_OF[a], lane)

    def plane(ref, at):
        down = 8 + (at >= PLANES) - (at < 0)
        return ref[at % PLANES, down : down + GROUPS]

    north = turn(jnp.where(lane >= LANES - 16, plane(tn, a + 1), plane(tn, a + 2)), 16)
    south = turn(jnp.where(lane < 16, plane(ts, a - 1), plane(ts, a - 2)), -16)
    return east + west + north + south


def choose(planes, lane, get):
    value = get(planes[0])
    for j in range(1, GROUP):
        low = (OFF[j] - (32 if planes is LAST else 0)) % LANES
        value = jnp.where(jnp.logical_and(lane >= low, lane < low + 16), get(planes[j]), value)
    return value


def forcing_kernel(
    levels, per, tiles_x, tiles_y,
    pos_in, temp_in, zonal_in, merid_in, depth_in, ocean_in, diag_in, source_in,
    fields, slots_out, around,
    temp, zonal, merid, depth, ocean, source, slots,
    st, sx, sy, pt, te, tw, tn, ts, edges, pos, holder, sems, out_sems,
):
    count = pos.shape[0]
    steps = levels // per
    number_pieces, runs = pieces_of(levels, count)
    slot = RIM_ROWS + number_pieces
    pairs = []
    for step in range(steps):
        chunk = pl.ds(step * per * ROWS, per * ROWS)
        pairs += [
            (a.at[chunk], b.at[chunk]) for a, b in ((temp_in, temp), (zonal_in, zonal), (merid_in, merid))
        ]
    pairs += [
        (a.reshape(ROWS, LANES), b)
        for a, b in (
            (source_in, source), (ocean_in, ocean), (depth_in, depth),
            (diag_in, fields.at[pl.ds(2 * HELD, ROWS)]),
        )
    ]
    copies = fetching([(pos_in, pos)] + pairs, sems)
    copies.pop(0).wait()
    results = []

    def send(value, target):
        copy = pltpu.make_async_copy(value, target, out_sems.at[len(results)])
        copy.start()
        results.append(copy)

    lane = lane_of((GROUPS, LANES))
    one = lane_of((1, LANES))
    q = lane % 16
    edges[...] = jnp.zeros_like(edges)

    def number(d, carry):
        holder[pos[d]] = d
        return carry

    lax.fori_loop(0, count, number, 0)
    me = lax.axis_index("gx") * tiles_y + lax.axis_index("gy")
    here = pos[me]
    row = here // tiles_x
    column = here % tiles_x
    sides = []
    for c, (dx, dy) in enumerate(SIDES):
        there = row + dy
        inside = jnp.logical_and(there >= 0, there < tiles_y)
        target = jnp.where(inside, there, 0) * tiles_x + (column + dx + tiles_x) % tiles_x
        device = jnp.where(inside, holder[target], -1)
        around[4 * count + c] = device
        sides.append(device)

    def look(y, carry):
        line = [holder[y * tiles_x + x] for x in range(tiles_x)]
        below = [holder[jnp.maximum(y - 1, 0) * tiles_x + x] for x in range(tiles_x)]
        above = [holder[jnp.minimum(y + 1, tiles_y - 1) * tiles_x + x] for x in range(tiles_x)]
        for x, device in enumerate(line):
            for c, other in enumerate((line[x - 1], line[(x + 1) % tiles_x], below[x], above[x])):
                around[c * count + device] = other * slot + RIM_ROWS
        return carry

    lax.fori_loop(0, tiles_y, look, 0)
    clear_terms(tn, ts)

    def add(flats, low, size, fresh):
        rows = pl.ds(low, size)
        total = [None] * 3
        for t, u, v in zip(*flats):
            t = t.rows(low, size)
            new = (t, t * u.rows(low, size), t * v.rows(low, size))
            total = [b if a is None else a + b for a, b in zip(total, new)]
        for ref, value in zip((st, sx, sy), total):
            ref[rows, :] = value if fresh else ref[rows, :] + value

    for step in range(steps):
        for copy in copies[3 * step : 3 * step + 3]:
            copy.wait()
        flats = [
            [Level(ref, (step * per + n) * ROWS) for n in range(per)] for ref in (temp, zonal, merid)
        ]

        def some(m, carry):
            add(flats, pl.multiple_of(m * 8, 8), 8, step == 0)
            return carry

        lax.fori_loop(0, ROWS // 8, some, 0, unroll=4)
        if ROWS % 8:
            add(flats, ROWS - ROWS % 8, ROWS % 8, step == 0)

        for n in range(per):
            k = step * per + n
            t, u, v = (flat[n] for flat in flats)

            loaded = {a: (t.plane(a), u.plane(a)) for a in sorted(set(START + LAST))}

            def term(planes, sign):
                own = choose(planes, lane, lambda a: loaded[a][0])
                flow = choose(planes, lane, lambda a: loaded[a][1])
                return DIFFUSE * own + sign * ADVECT * (flow * own)

            edges[0, 0:GROUPS] = jnp.where(q == k, turn(term(START, -1.0), k), edges[0, 0:GROUPS])
            edges[1, 0:GROUPS] = jnp.where(q == k, turn(term(LAST, 1.0), k + 17), edges[1, 0:GROUPS])
            rows = t.rows(0, 2)
            rows = DIFFUSE * rows - ADVECT * (v.rows(0, 2) * rows)
            edges[2, k : k + 1] = rows[0:1]
            edges[2, k + levels : k + levels + 1] = rows[1:2]
            rows = t.rows(ROWS - 2, 2)
            rows = DIFFUSE * rows + ADVECT * (v.rows(ROWS - 2, 2) * rows)
            edges[3, k : k + 1] = turn(jnp.where(one >= 16, rows[0:1], rows[1:2]), -16)
            edges[3, k + levels : k + levels + 1] = turn(rows[1:2], -16)

    for c in range(4):
        for j, device, low, size in runs[c]:
            slots[pl.ds(device * slot + RIM_ROWS + j, size, stride=slot), :] = edges[c, low : low + size]

    for copy in copies[3 * steps :]:
        copy.wait()

    part = fields.at[pl.ds(0, HELD)]
    mask = fields.at[pl.ds(HELD, HELD)]
    diag = fields.at[pl.ds(2 * HELD, HELD)]
    own = fields.at[pl.ds(PACKS, 56)]
    mask[0:ROWS] = depth[...] * ocean[...].astype(jnp.float32)

    def wet_of(rows):
        return ocean[rows, :].astype(jnp.float32)

    def masked(rows):
        return mask[rows, :]

    for a in range(PLANES):
        total = st[comb(a), :]
        pt[a] = total
        store_terms(a, total, ADVECT * sx[comb(a), :], ADVECT * sy[comb(a), :], te, tw, tn, ts)
    for a in range(PLANES):
        total = pt[a]
        wet = wet_of(comb(a))
        change = inner_sum(a, te, tw, tn, ts) - 4.0 * DIFFUSE * total
        part[comb(a), :] = source[comb(a), :] + (STERIC / levels) * wet * (total + wet * change)

    def mix(*values):
        value = values[-1]
        for at, low in ((6, 12), (5, 11), (4, 10), (3, 9), (2, 8), (1, 6), (0, 3)):
            value = jnp.where(q < low, values[at], value)
        return value

    def ends(planes, low):
        value = tn[planes[0], 8 : 8 + GROUPS]
        last = jnp.logical_and(lane >= low, lane < low + 16)
        return jnp.where(last, ts[planes[7], 8 : 8 + GROUPS], value)

    def beside(b, d, g, b_out, d_out):
        return g * b + d * d_out * (b - b_out)

    bp = choose(START, lane, lambda a: part[comb(a), :])
    dp = choose(START, lane, lambda a: masked(comb(a)))
    gp = choose(START, lane, lambda a: diag[comb(a), :])
    pp = beside(bp, dp, gp, turn(bp, -1), turn(dp, -1))
    pack_w = mix(
        bp, turn(dp, 3), turn(gp, 6), turn(pp, 6), turn(choose(START, lane, lambda a: te[a]), 9),
        turn(gp, 8), turn(dp, 8), turn(ends(START, OFF[7]), 12),
    )
    bp = choose(LAST, lane, lambda a: part[comb(a), :])
    dp = choose(LAST, lane, lambda a: masked(comb(a)))
    gp = choose(LAST, lane, lambda a: diag[comb(a), :])
    pp = beside(bp, dp, gp, turn(bp, 1), turn(dp, 1))
    pack_e = mix(
        turn(bp, 19), turn(dp, 22), turn(gp, 24), turn(pp, 27),
        turn(choose(LAST, lane, lambda a: tw[a]), 26),
        turn(gp, 29), turn(dp, 31), turn(ends(LAST, LANES - 16), 32),
    )
    own[0:GROUPS] = pack_w
    own[SLABS : SLABS + GROUPS] = pack_e
    north_l = tn[0, 8:9]
    north_r = tn[1, 8:9]
    south_13 = ts[PLANES - 2, 7 + GROUPS : 8 + GROUPS]
    south_14 = ts[PLANES - 1, 7 + GROUPS : 8 + GROUPS]
    south_l = turn(jnp.where(one >= 16, south_13, south_14), -16)
    south_r = turn(south_14, -16)
    own[48:49] = north_l
    own[49:50] = north_r
    own[50:51] = south_l
    own[51:52] = south_r
    deep = jnp.max(masked(slice(0, ROWS)), axis=(0, 1), keepdims=True)
    top = jnp.max(diag[0:ROWS], axis=(0, 1), keepdims=True) + 8.0 * deep * deep
    top = jnp.broadcast_to(top, (1, LANES))

    slots[pl.ds(RIM_ROWS - 1, count, stride=slot), :] = jnp.broadcast_to(top, (count, LANES))
    block_lane = lane_of((6, LANES))
    block_row = row_of((6, LANES))
    for c, first, rows_l, rows_r in ((2, True, north_l, north_r), (3, False, south_l, south_r)):
        base = 0 if first else ROWS - 6
        if first:
            spare = jnp.logical_and(block_row == 5, block_lane >= 80)
        else:
            spare = jnp.logical_and(block_row == 0, block_lane < 48)
        g = 0 if first else GROUPS - 1
        blocks = []
        block = slice(base, base + 6)
        for value, at in ((part[block, :], g), (masked(block), SLABS + g)):
            extra = jnp.broadcast_to(turn(own[at : at + 1], -16), (6, LANES))
            blocks.append(jnp.where(spare, extra, value))
        low = 0 if first else ROWS - 4
        diag_rows = diag[low : low + 4, :]
        third, fourth = (2, 3) if first else (SPAN_Y - 3, SPAN_Y - 4)
        b_l, b_r = line_of(lambda n: part[n : n + 1, :], third)
        d_l, d_r = line_of(lambda n: masked(slice(n, n + 1)), third)
        g_l, g_r = line_of(lambda n: diag[n : n + 1, :], third)
        bo_l, bo_r = line_of(lambda n: part[n : n + 1, :], fourth)
        do_l, do_r = line_of(lambda n: masked(slice(n, n + 1)), fourth)
        out_l = beside(b_l, d_l, g_l, bo_l, do_l)
        out_r = beside(b_r, d_r, g_r, bo_r, do_r)
        for at, value in ((112, turn(g_l, 112)), (113, turn(do_l, 113)), (114, turn(g_r, 3)), (115, turn(do_r, 4))):
            out_r = jnp.where(one == at, value, out_r)
        last_row = jnp.where(one == LANES - 1, top, rows_r)

        @pl.when(sides[c] >= 0)
        def _(c=c, blocks=blocks, diag_rows=diag_rows, singles=(out_l, out_r, rows_l, last_row)):
            at = sides[c] * slot
            slots[pl.ds(at, 6), :] = blocks[0]
            slots[pl.ds(at + 6, 6), :] = blocks[1]
            slots[pl.ds(at + 12, 4), :] = diag_rows
            for n, value in enumerate(singles):
                slots[pl.ds(at + 16 + n, 1), :] = value

    corner = jnp.logical_and(row_of((GROUPS, LANES)) == RIM_ROWS - 1, lane == LANES - 1)
    for c, pack in ((0, pack_w), (1, pack_e)):
        slots[pl.ds(sides[c] * slot, GROUPS), :] = jnp.where(corner, top, pack)
    for c, at in ((4, 0), (5, SLABS), (6, GROUPS - 1), (7, SLABS + GROUPS - 1)):
        @pl.when(sides[c] >= 0)
        def _(c=c, at=at):
            slots[pl.ds(sides[c] * slot, 1), :] = own[at : at + 1]
    send(slots, slots_out.reshape(count * slot, LANES))
    for copy in results:
        copy.wait()


SMEM = pl.BlockSpec(memory_space=pltpu.SMEM)


def solve_kernel(
    levels, tiles_y,
    around_in, rims, fields,
    vectors, hands,
    around, sem, north_in, south_in, fb, fd, fg, pw, pe, ow, oe, ed, eg, ex, we, wn, last, rows,
):
    copies = fetching([(around_in, around)], sem)
    count = rims.shape[0]
    number_pieces, _ = pieces_of(levels, count)
    slot = RIM_ROWS + number_pieces
    share = 1 + number_pieces
    came = rims.reshape(count * slot, LANES)
    hand = hands.reshape(count * share, LANES)
    own = fields.at[pl.ds(PACKS, 56)]
    lane = lane_of((SLABS, LANES))
    slab = row_of((SLABS, LANES))
    one = lane_of((1, LANES))

    none = jnp.zeros((WIDE - ROWS + 4, LANES), jnp.float32)
    for ref in (fb, fd, fg):
        ref[ROWS - 4 : WIDE] = none
    for n, ref in enumerate((fb, fd, fg)):
        ref[0:ROWS] = fields[n * HELD : n * HELD + ROWS]
    copies[0].wait()
    src = [around[4 * count + c] for c in range(8)]

    def fetch(c, low, high):
        value = came[pl.ds(jnp.maximum(src[c], 0) * slot + low, high - low), :]
        return jnp.where(src[c] >= 0, value, 0.0)

    me = lax.axis_index("gx") * tiles_y + lax.axis_index("gy")
    for n in range(number_pieces):
        side = jnp.minimum((n * count + me) // (2 * levels), 3)
        base = (side + 1 - 2 * (side % 2)) * count

        def relay(d, carry, n=n, base=base):
            row = around[base + d] + n
            hand[pl.ds(d * share + 1 + n, 1), :] = came[pl.ds(row, 1), :]
            return carry

        for d in range(count):
            relay(d, 0)

    north_in[0:RIM_ROWS] = fetch(3, 0, RIM_ROWS)
    south_in[0:RIM_ROWS] = fetch(2, 0, RIM_ROWS)
    strips = {2: south_in, 3: north_in}
    for ref, low, high, n_lane, s_lane in ((fb, 0, 6, 80, 48), (fd, 6, 12, 80, 48), (fg, 12, 16, 96, 32)):
        size = high - low
        row, column = row_of((size, LANES)), lane_of((size, LANES))
        beyond = jnp.logical_and(row == size - 1, column >= n_lane)
        ref[ROWS : ROWS + size] = jnp.where(beyond, 0.0, strips[3][low:high])
        beyond = jnp.logical_and(row == 0, column < s_lane)
        ref[WIDE - size : WIDE] = jnp.where(beyond, 0.0, strips[2][low:high])
    empty = jnp.zeros((SLABS, LANES), jnp.float32)
    for ref, side, north, south in ((pw, 0, 6, 4), (pe, 1, 7, 5)):
        ref[...] = empty
        ref[0:GROUPS] = fetch(side, 0, GROUPS)
        ref[GROUPS : GROUPS + 1] = fetch(north, 0, 1)
        ref[SLABS - 1 : SLABS] = fetch(south, 0, 1)
    for ref, at, north, south in ((ow, 0, 5, 0), (oe, SLABS, 11, 6)):
        ref[...] = empty
        ref[0:GROUPS] = own[at : at + GROUPS]
        ref[GROUPS : GROUPS + 1] = turn(strips[3][north:north + 1], 16)
        ref[SLABS - 1 : SLABS] = turn(strips[2][south:south + 1], 16)

    def spread(ref, j):
        a = START[j]
        first, second = ref[comb(a, SLABS), :], ref[comb(a + 1, SLABS), :]
        third = ref[comb(a + 2, SLABS), :] if a + 2 < PLANES else second
        left = turn(jnp.where(lane >= OFF[j], first, second), -OFF[j])
        right = turn(jnp.where(lane >= OFF[j], second, third), -OFF[j])
        return left, right

    def seam_row(left, right, slab_at, lanes_at):
        east = turn(pe[slab_at : slab_at + 1], 112 - lanes_at)
        west = turn(pw[slab_at : slab_at + 1], 124 - lanes_at)
        right = jnp.where(one < 112, right, jnp.where(one < 116, east, jnp.where(one >= 124, west, 0.0)))
        return jnp.broadcast_to(left, (SLABS, LANES)), jnp.broadcast_to(right, (SLABS, LANES))

    seams = {
        0: ((0, seam_row(strips[2][18:19], strips[2][19:20], SLABS - 1, 28)),
            (GROUPS, seam_row(own[50:51], own[51:52], GROUPS - 1, 28))),
        GROUP - 1: ((GROUPS - 1, seam_row(strips[3][18:19], strips[3][19:20], GROUPS, 12)),
                    (SLABS - 1, seam_row(own[48:49], own[49:50], 0, 12))),
    }
    weight = STERIC / levels

    def missing(target, term, term_out, d, d_out, g):
        term, term_out, d, d_out, g = (
            turn(value[0], target - value[1]) for value in (term, term_out, d, d_out, g)
        )
        term = jnp.where(d > 0, weight * term, 0.0)
        term_out = jnp.where(d_out > 0, weight * term_out, 0.0)
        return jnp.where(one == target, g * term + d * d_out * (term - term_out), 0.0)

    def ring(ref, at):
        return ref[at : at + 1]

    outer = {j: [] for j in range(GROUP)}
    for j, at, beyond, o, lanes in ((0, 0, SLABS - 1, 0, 28), (GROUP - 1, GROUPS - 1, GROUPS, 16, 12)):
        own_row, corner = ring(pe, at), ring(pe, beyond)
        outer[j].append((1, at, missing(
            114, (corner, lanes + 2), (corner, lanes + 3), (own_row, o + 5), (own_row, o + 11), (own_row, o + 10),
        )))
        own_row, corner = ring(pw, at), ring(pw, beyond)
        outer[j].append((1, at, missing(
            125, (corner, lanes + 1), (corner, lanes), (own_row, o + 3), (own_row, o + 11), (own_row, o + 10),
        )))
    for j, at, c, j_out, d_l, d_r in ((2, GROUPS, 3, 3, (9, 96), (11, 79)), (5, SLABS - 1, 2, 4, (6, 48), (8, 31))):
        line_l, line_r = strips[c][16:17], strips[c][17:18]
        corner = ring(pw, at)
        outer[j].append((0, at, line_l + missing(
            0, (corner, OFF[j] + 9), (corner, OFF[j_out] + 9), (strips[c][d_l[0]:d_l[0] + 1], d_l[1]),
            (line_r, 113), (line_r, 112),
        )))
        corner = ring(pe, at)
        outer[j].append((1, at, jnp.where(one < 112, line_r, 0.0) + missing(
            111, (corner, OFF[j] + 9), (corner, OFF[j_out] + 9), (strips[c][d_r[0]:d_r[0] + 1], d_r[1]),
            (line_r, 115), (line_r, 114),
        )))
    for j in range(GROUP):
        o = OFF[j]
        inside = slab < GROUPS
        halves = [
            jnp.zeros((SLABS, LANES), jnp.float32),
            jnp.where(
                jnp.logical_and(inside, lane == 114), turn(pe[...], 114 - o - 8),
                jnp.where(jnp.logical_and(inside, lane == 125), turn(pw[...], 125 - o - 8), 0.0),
            ),
        ]
        for half, at, line in outer[j]:
            halves[half] = halves[half] + jnp.where(slab == at, line, 0.0)
        ex[j, :, 0:LANES] = halves[0]
        ex[j, :, LANES:] = halves[1]

        def rim(right, q, width):
            east = turn(pe[...], 112 - o - q)
            west = turn(pw[...], 128 - width - o - q)
            value = jnp.where(lane < 112 + width, east, jnp.where(lane >= 128 - width, west, 0.0))
            return jnp.where(lane < 112, right, value)

        left, right = spread(fd, j)
        right = rim(right, 3, 3)
        wet_l = jnp.where(left > 0, weight, 0.0)
        wet_r = jnp.where(right > 0, weight, 0.0)
        ed[j, :, 0:LANES] = left
        ed[j, :, LANES:] = right
        left, right = spread(fg, j)
        eg[j, :, 0:LANES] = left
        eg[j, :, LANES:] = rim(right, 6, 2)
        left, right = spread(fb, j)
        right = rim(right, 0, 3)
        seam_l = jnp.where(lane == 0, turn(pw[...], -o - 9), 0.0)
        seam_r = jnp.where(lane == 127, turn(ow[...], 127 - o - 9), 0.0)
        seam_r = jnp.where(lane == 111, turn(pe[...], 111 - o - 9), seam_r)
        seam_r = jnp.where(lane == 112, turn(oe[...], 112 - o - 9), seam_r)
        for at, (row_l, row_r) in seams.get(j, ()):
            seam_l = seam_l + jnp.where(slab == at, row_l, 0.0)
            seam_r = seam_r + jnp.where(slab == at, row_r, 0.0)
        vectors[0, j, :, 0:LANES] = left + wet_l * seam_l
        vectors[0, j, :, LANES:] = right + wet_r * seam_r

    for j in range(GROUP):
        d = ed[j]
        we[j] = d * turn(d, -1)
        above = ed[j + 1] if j < GROUP - 1 else turn(ed[0], -1, 0)
        wn[j] = d * above

    top = jnp.max(came[pl.ds(RIM_ROWS - 1, count, stride=slot), :], axis=0, keepdims=True)
    top = jnp.max(jnp.where(one == LANES - 1, top, 0.0), axis=1, keepdims=True)
    scale = STRETCH / top

    big = (SLABS, 2 * LANES)
    mine = jnp.logical_and(row_of(big) < GROUPS, lane_of(big) < SPAN_X)
    pair = 0
    for k in range(5):
        sums = [None] * (k + 1)
        new = last if k == 4 else vectors.at[k]
        if k:
            v = vectors.at[k - 1]
            flow_below = wn[GROUP - 1] * (v[GROUP - 1] - turn(v[0], -1, 0))
            flow_below = turn(flow_below, 1, 0)
        for j in range(GROUP):
            if k:
                here = v[j]
                above = v[j + 1] if j < GROUP - 1 else turn(v[0], -1, 0)
                flow_x = we[j] * (here - turn(here, -1))
                flow_y = wn[j] * (here - above)
                image = eg[j] * here + (flow_x - turn(flow_x, 1)) + (flow_y - flow_below)
                if k == 1:
                    image = image + ex[j]
                fresh = scale * image - (STRETCH * ROOTS[k - 1]) * here
                flow_below = flow_y
                new[j] = fresh
            else:
                fresh = new[j]
            held = jnp.where(mine, fresh, 0.0)
            for i in range(k + 1):
                other = vectors[i, j] if i < k else held
                value = held * other
                sums[i] = value if sums[i] is None else sums[i] + value
        for i in range(k + 1):
            rows[pair : pair + 1] = jnp.sum(sums[i][:, 0:LANES] + sums[i][:, LANES:], axis=0, keepdims=True)
            pair += 1
    rows[pair : pair + 1] = jnp.where(one == 0, top, 0.0)
    total = jnp.sum(rows[...], axis=1, keepdims=True)
    spot = row_of((16, LANES)) == lane_of((16, LANES))
    line = jnp.sum(jnp.where(spot, total, 0.0), axis=0, keepdims=True)
    hand[pl.ds(0, count, stride=share), :] = jnp.broadcast_to(line, (count, LANES))


def finish_kernel(
    levels, per, hands, vectors, edges, inner, tracer_out, surface_out,
    cells, flat, left, right, message, out_sems,
):
    count = hands.shape[0]
    number_pieces, runs = pieces_of(levels, count)
    share = 1 + number_pieces
    came = hands.reshape(count * share, LANES)
    steps = levels // per
    chunks = [pl.ds(step * per * ROWS, per * ROWS) for step in range(steps)]
    row = jnp.sum(came[pl.ds(0, count, stride=share), :], axis=0, keepdims=True)
    one = lane_of((1, LANES))
    entry = {}
    pair = 0
    for k in range(5):
        for i in range(k + 1):
            value = jnp.sum(jnp.where(one == pair, row, 0.0), axis=1, keepdims=True)
            entry[i, k] = entry[k, i] = value
            pair += 1
    top = jnp.sum(jnp.where(one == pair, row, 0.0), axis=1, keepdims=True) * (1.0 / count)

    def image(c):
        out = [None] * 5
        for k in range(4):
            if c[k] is None:
                continue
            low = ROOTS[k] * c[k]
            out[k] = low if out[k] is None else out[k] + low
            out[k + 1] = (1.0 / STRETCH) * c[k]
        return out

    def dot(a, b):
        total = None
        for i in range(5):
            if a[i] is None:
                continue
            inner = None
            for j in range(5):
                if b[j] is not None:
                    value = entry[i, j] * b[j]
                    inner = value if inner is None else inner + value
            total = a[i] * inner if total is None else total + a[i] * inner
        return total

    def axpy(a, s, b):
        return [
            x if y is None else (s * y if x is None else x + s * y) for x, y in zip(a, b)
        ]

    r = [jnp.ones((1, 1), jnp.float32)] + [None] * 4
    p = list(r)
    x = [None] * 5
    rr = entry[0, 0]
    for n in range(ITERS):
        q = image(p)
        step = rr / jnp.maximum(dot(p, q), TINY)
        step = jnp.clip(step, top * (1.0 / HIGH_RATE), top * (1.0 / LOW_RATE))
        x = axpy(x, step, p)
        if n < ITERS - 1:
            r = axpy(r, -step, q)
            fresh = jnp.maximum(dot(r, r), 0.0)
            p = axpy(r, fresh / jnp.maximum(rr, TINY), p)
            rr = fresh
    factors = [c / top for c in x[:4]]
    for j in range(GROUP):
        value = None
        for k in range(4):
            term = factors[k] * vectors[k, j]
            value = term if value is None else value + term
        left[j] = turn(value[:, 0:LANES], OFF[j])
        right[j] = turn(value[:, LANES:], OFF[j])
    lane = lane_of((SLABS, LANES))
    for a in range(PLANES):
        value = None
        for j in range(GROUP):
            for half, ref in ((0, left), (1, right)):
                low = max(SPAN_X * j + LANES * half - LANES * a, 0)
                high = min(SPAN_X * j + (LANES if half == 0 else SPAN_X) - LANES * a, LANES)
                if low >= high:
                    continue
                value = ref[j] if value is None else jnp.where(lane >= low, ref[j], value)
        flat[comb(a), :] = value[0:GROUPS]
    results = [pltpu.make_async_copy(flat, surface_out.reshape(ROWS, LANES), out_sems.at[0])]
    results[0].start()

    for c in range(4):
        for j, device, low, size in runs[c ^ 1]:
            value = came[pl.ds(device * share + 1 + j, size, stride=share), :]
            message[c, low : low + size] = value
    second = lane_of((SLABS, LANES)) % 16 == 1
    sums = []
    for k in range(levels):
        value = edges[2 * levels - 1] * jnp.concatenate([
            jnp.where(second, turn(message[1], 1 - k), turn(message[0], -k)),
            message[2, k : k + 1], message[2, k + levels : k + levels + 1],
            message[3, k : k + 1], message[3, k + levels : k + levels + 1],
            jnp.zeros((EDGE - SLABS - 4, LANES), jnp.float32),
        ], axis=0)
        if k:
            value = value + edges[2 * levels + k - 1] * sums[-1]
        sums.append(value * edges[levels - 1 + k])
    for k in range(levels - 2, -1, -1):
        sums[k] = sums[k] + edges[k] * sums[k + 1]
    lane = lane_of((GROUPS, LANES))
    slab = row_of((GROUPS, LANES))
    for k in range(levels):
        west = sums[k][0:GROUPS]
        east = turn(west, -18)
        south_l, south_r = sums[k][SLABS : SLABS + 1], sums[k][SLABS + 1 : SLABS + 2]
        north_l = turn(sums[k][SLABS + 2 : SLABS + 3], 16)
        north_r = turn(sums[k][SLABS + 3 : SLABS + 4], 16)
        for a in range(PLANES):
            rim = None
            for at, source in [(at, west) for at in FIRST_OF[a]] + [(at, east) for at in LAST_OF[a]]:
                rim = jnp.where(lane == at, source, 0.0 if rim is None else rim)
            rows = comb(k * ROWS + a)
            if rim is None:
                cells[rows, :] = inner[rows, :]
                continue
            if a == 0:
                rim = rim + jnp.where(slab == 0, south_l, 0.0)
            if a == 1:
                rim = rim + jnp.where(jnp.logical_and(slab == 0, lane < 112), south_r, 0.0)
            if a == PLANES - 2:
                rim = rim + jnp.where(jnp.logical_and(slab == GROUPS - 1, lane >= 16), north_l, 0.0)
            if a == PLANES - 1:
                rim = rim + jnp.where(slab == GROUPS - 1, jnp.where(lane < 16, north_l, north_r), 0.0)
            cells[rows, :] = inner[rows, :] + rim
        if k % per == per - 1:
            step = k // per
            copy = pltpu.make_async_copy(
                cells.at[chunks[step]], tracer_out.at[chunks[step]], out_sems.at[1 + step]
            )
            copy.start()
            results.append(copy)
    for copy in results:
        copy.wait()


def tracer_kernel(
    levels, per, sides, around, temp_in, zonal_in, merid_in, rates_in, fields,
    out, edges,
    temp, zonal, merid, rates, ocean,
    te, tw, tn, ts, stepped, border, sems,
):
    steps = levels // per
    pairs = []
    for step in range(steps):
        chunk = pl.ds(step * per * ROWS, per * ROWS)
        pairs += [
            (a.at[chunk], b.at[chunk]) for a, b in ((temp_in, temp), (zonal_in, zonal), (merid_in, merid))
        ]
    copies = fetching(pairs + [(rates_in.reshape((levels - 1) * ROWS, LANES), rates)], sems)
    lane = lane_of((GROUPS, LANES))
    one = lane_of((1, LANES))
    clear_terms(tn, ts)

    ocean[...] = jnp.where(fields[HELD : HELD + ROWS] > 0, 1.0, 0.0)
    for step in range(steps):
        for copy in copies[3 * step : 3 * step + 3]:
            copy.wait()

        def level(k, carry):
            t, u, v = (Level(ref, k * ROWS) for ref in (temp, zonal, merid))
            for a in range(PLANES):
                own = t.plane(a)
                quarter = ADVECT * own
                store_terms(a, own, u.plane(a) * quarter, v.plane(a) * quarter, te, tw, tn, ts)
            for a in range(PLANES):
                own = t.plane(a)
                change = inner_sum(a, te, tw, tn, ts) - 4.0 * DIFFUSE * own
                stepped[k, a] = own + ocean[comb(a), :] * change
            return carry

        lax.fori_loop(step * per, step * per + per, level, 0)
    copies[-1].wait()

    def block(a, carry):
        for low in range(0, GROUPS, 8):
            size = min(8, GROUPS - low)

            def rows(k):
                return pl.ds(k * ROWS + low * PLANES + a, size, stride=PLANES)

            gains = []
            sums = []
            for k in range(levels):
                value = stepped[k, a, low : low + size]
                pivot = 1.0
                if k > 0:
                    pivot = pivot + upper - upper * gains[-1]
                    value = value + upper * sums[-1]
                if k < levels - 1:
                    lower = rates[rows(k), :]
                    inverse = 1.0 / (pivot + lower)
                    gains.append(lower * inverse)
                    upper = lower
                else:
                    inverse = 1.0 / pivot
                sums.append(value * inverse)
            result = sums[-1]
            out[rows(levels - 1), :] = result
            for k in range(levels - 2, -1, -1):
                result = sums[k] + gains[k] * result
                out[rows(k), :] = result
        return carry

    lax.fori_loop(0, PLANES, block, 0)

    def edge(ref, base, at):
        def get(a):
            return ref[comb(base + a), :].astype(jnp.float32)

        border[0:GROUPS] = jnp.where(
            lane % 16 == 1, turn(choose(LAST, lane, get), 18), choose(START, lane, get)
        )
        border[SLABS : SLABS + 2] = ref[base : base + 2, :].astype(jnp.float32)
        rows = ref[base + ROWS - 2 : base + ROWS, :].astype(jnp.float32)
        border[SLABS + 2 : SLABS + 3] = turn(jnp.where(one >= 16, rows[0:1], rows[1:2]), -16)
        border[SLABS + 3 : SLABS + 4] = turn(rows[1:2], -16)
        edges[at] = border[...]

    border[...] = jnp.zeros_like(border)
    edge(ocean, 0, 2 * levels - 1)
    for c in (2, 3):
        rows = pl.ds(SLABS + 2 * (c - 2), 2)
        value = edges[2 * levels - 1, rows]
        edges[2 * levels - 1, rows] = jnp.where(around[sides + c] >= 0, value, 0.0)
    gain = None
    for k in range(levels):
        pivot = 1.0
        if k > 0:
            upper = edges[2 * levels + k - 1]
            pivot = pivot + upper - upper * gain
        if k < levels - 1:
            edge(rates, k * ROWS, 2 * levels + k)
            lower = edges[2 * levels + k]
            inverse = 1.0 / (pivot + lower)
            gain = lower * inverse
            edges[k] = gain
        else:
            inverse = 1.0 / pivot
        edges[levels - 1 + k] = inverse


def on_device(
    thermal_anomaly,
    zonal_flow_ratio,
    meridional_flow_ratio,
    diffusion_rates,
    ocean_bottom_scaled,
    ocean_indicator,
    operator_diagonal,
    elevation_source,
    block_positions,
):
    levels, cells = thermal_anomaly.shape[1:]
    nx = lax.axis_size("gx")
    ny = lax.axis_size("gy")
    count = block_positions.shape[0]
    planes = (ocean_bottom_scaled, ocean_indicator, operator_diagonal, elevation_source)
    depth, ocean, diag, source = planes
    f32 = jnp.float32
    per = next(n for n in (4, 2, 6, levels) if levels % n == 0 and n * ROWS % 8 == 0)
    steps = levels // per
    few = next(n for n in (2, 4, 6, levels) if levels % n == 0 and n * ROWS % 8 == 0)
    params = pltpu.CompilerParams(vmem_limit_bytes=BUDGET)
    temp, zonal, merid = (
        array.reshape(levels * ROWS, LANES)
        for array in (thermal_anomaly, zonal_flow_ratio, meridional_flow_ratio)
    )
    rates = diffusion_rates.reshape(levels - 1, 1, cells)
    temp, zonal, merid, rates, depth, ocean, diag, source, positions = (
        pltpu.with_memory_space_constraint(array, pltpu.HBM)
        for array in (temp, zonal, merid, rates, depth, ocean, diag, source, block_positions)
    )
    hbm = pl.BlockSpec(memory_space=pltpu.HBM)
    here = pl.BlockSpec(memory_space=pltpu.VMEM)

    def vmem(*shape, kind=f32):
        return pltpu.VMEM(shape, kind)

    def out(*shape, kind=f32):
        return jax.ShapeDtypeStruct(shape, kind)

    def sems(number):
        return pltpu.SemaphoreType.DMA((number,))

    deep = vmem(levels * ROWS, LANES)
    flat = vmem(ROWS, LANES)
    flat_int = vmem(ROWS, LANES, kind=jnp.int32)
    plane = vmem(PLANES, GROUPS, LANES)
    tall = vmem(PLANES, 40, LANES)
    numbers = pltpu.SMEM((count,), jnp.int32)
    number_pieces, _ = pieces_of(levels, count)
    slot = RIM_ROWS + number_pieces
    share = 1 + number_pieces
    fields, slots, around = pl.pallas_call(
        functools.partial(forcing_kernel, levels, few, nx, ny),
        in_specs=[hbm] * 8,
        out_specs=[here, hbm, SMEM],
        out_shape=[
            out(FIELDS, LANES), pltpu.HBM((count, 1, slot * LANES), f32), out(4 * count + 8, kind=jnp.int32),
        ],
        scratch_shapes=[deep] * 3 + [flat, flat_int, flat]
        + [vmem(count * slot, LANES)]
        + [flat] * 3 + [plane] * 3 + [tall] * 2
        + [vmem(4, 2 * levels, LANES), numbers, numbers, sems(3 * (levels // few) + 5), sems(1)],
        compiler_params=params,
        name="forcing",
    )(positions, temp, zonal, merid, depth, ocean, diag, source)
    rims = lax.all_to_all(slots, BOTH, 0, 0, tiled=True)

    inner, edges = pl.pallas_call(
        functools.partial(tracer_kernel, levels, per, 4 * count),
        in_specs=[SMEM] + [hbm] * 4 + [here],
        out_specs=[here] * 2,
        out_shape=[out(levels * ROWS, LANES), out(3 * levels - 1, EDGE, LANES)],
        scratch_shapes=[deep] * 3 + [vmem((levels - 1) * ROWS, LANES), flat]
        + [plane] * 2 + [tall] * 2
        + [vmem(levels, PLANES, GROUPS, LANES), vmem(EDGE, LANES), sems(3 * steps + 1)],
        compiler_params=params,
        name="tracer",
    )(around, temp, zonal, merid, rates, fields)

    rims, edges = lax.optimization_barrier((rims, edges))
    extended = vmem(GROUP, SLABS, 2 * LANES)
    vectors, hand = pl.pallas_call(
        functools.partial(solve_kernel, levels, ny),
        in_specs=[pl.BlockSpec(memory_space=pl.ANY)] + [here] * 2,
        out_specs=[here] * 2,
        out_shape=[out(4, GROUP, SLABS, 2 * LANES), out(count, 1, share * LANES)],
        scratch_shapes=[pltpu.SMEM((4 * count + 8,), jnp.int32), sems(1)]
        + [vmem(SLABS, LANES)] * 2 + [vmem(WIDE, LANES)] * 3 + [vmem(SLABS, LANES)] * 4 + [extended] * 6 + [vmem(16, LANES)],
        compiler_params=params,
        name="vectors",
    )(around, rims, fields)
    hands = lax.all_to_all(hand, BOTH, 0, 0, tiled=True)

    new_temp, surface = pl.pallas_call(
        functools.partial(finish_kernel, levels, per),
        in_specs=[here] * 4,
        out_specs=[hbm] * 2,
        out_shape=[out(levels * ROWS, LANES), out(1, cells)],
        scratch_shapes=[
            deep, flat, vmem(GROUP, SLABS, LANES), vmem(GROUP, SLABS, LANES), vmem(4, 2 * levels, LANES),
            sems(1 + steps),
        ],
        compiler_params=params,
        name="finish",
    )(hands, vectors, edges, inner)
    return new_temp.reshape(1, levels, cells), surface


def solution(mesh):
    deep = P(BOTH, None, None)
    flat = P(BOTH, None)
    return jax.shard_map(
        on_device,
        mesh=mesh,
        in_specs=(deep, deep, deep, deep, flat, flat, flat, flat, P()),
        out_specs=(deep, flat),
        check_vma=False,
    )
```

profile of v0, /device:TPU:0, one launch (start us, length us, event | category | flops | bytes accessed | tf_op | source)
XLA Modules:
  0.0 39.6 jit_solution(12530204636530028130)
XLA Ops:
  0.6 5.0 %forcing.1 = (f32[968,128]{1,0:T(8,128)S(1)}, f32[32,1,2944]{2,1,0:T(1,128)}, s32[136]{0:T(256)S(1)}) custom-call(s32[32]{0:T(128)} %pos_in.1, f32[3600,128]{1,0:T(8,128)} %bitcast.5, f32[3600,128]{1,0:T(8,128)} %bitcast.7, f32[3600,128]{1,0:T(8,128)} %bitcast.9, f32[1,38400]{1,0:T(1,128)} %depth_in.1, s32[1,38400]{1,0:T(1,128)} %ocean_in.1, ...), custom_call_target="tpu_custom_call" | custom-call | tf_op jit(solution)/shard_map/forcing/pallas_call | solution.py:903
  5.7 7.3 %all-to-all-start = ((f32[32,1,2944]{2,1,0:T(1,128)}), f32[32,1,2944]{2,1,0:T(1,128)S(1)}, u32[]{:S(2)}, u32[]{:S(2)}) async-start(f32[32,1,2944]{2,1,0:T(1,128)} %get-tuple-element.14), calls=%async_computation | async-start | bytes 753664 | tf_op jit(solution)/shard_map/all_to_all | solution.py:917
  12.9 8.0 %tracer.1 = (f32[3600,128]{1,0:T(8,128)S(1)}, f32[35,32,128]{2,1,0:T(8,128)S(1)}) custom-call(s32[136]{0:T(256)S(1)} %get-tuple-element.13.around.around_in, f32[3600,128]{1,0:T(8,128)} %bitcast.6, f32[3600,128]{1,0:T(8,128)} %bitcast.8, f32[3600,128]{1,0:T(8,128)} %bitcast.10, f32[11,1,38400]{2,1,0:T(1,128)} %bitcast.11, ...), custom_call_target="tpu_custom_call" | custom-call | tf_op jit(solution)/shard_map/tracer/pallas_call | solution.py:919
  20.9 3.6 %all-to-all-done.rims = f32[32,1,2944]{2,1,0:T(1,128)S(1)} async-done(((f32[32,1,2944]{2,1,0:T(1,128)}), f32[32,1,2944]{2,1,0:T(1,128)S(1)}, u32[]{:S(2)}, u32[]{:S(2)}) %all-to-all-start) | async-done | bytes 376864 | tf_op jit(solution)/shard_map/all_to_all | solution.py:917
  24.5 2.2 %vectors.1 = (f32[4,8,24,256]{3,2,1,0:T(8,128)S(1)}, f32[32,1,512]{2,1,0:T(1,128)S(1)}) custom-call(s32[136]{0:T(256)S(1)} %get-tuple-element.13.around.around_in, f32[32,1,2944]{2,1,0:T(1,128)S(1)} %all-to-all-done.rims, f32[968,128]{1,0:T(8,128)S(1)} %get-tuple-element.15.fields), custom_call_target="tpu_custom_call" | custom-call | tf_op jit(solution)/shard_map/vectors/pallas_call | solution.py:933
  26.8 11.1 %all_to_all.10.hands = f32[32,1,512]{2,1,0:T(1,128)S(1)} all-to-all(f32[32,1,512]{2,1,0:T(1,128)S(1)} %get-tuple-element.18), channel_id=1, replica_groups=mesh['gx'=8,'gy'=4] {'gx','gy'}, dimensions={0} | all-to-all | bytes 131072 | tf_op jit(solution)/shard_map/all_to_all | solution.py:943
  37.8 1.8 %finish.1 = (f32[3600,128]{1,0:T(8,128)}, f32[1,38400]{1,0:T(1,128)}) custom-call(f32[32,1,512]{2,1,0:T(1,128)S(1)} %all_to_all.10.hands, f32[4,8,24,256]{3,2,1,0:T(8,128)S(1)} %get-tuple-element.19.vectors, f32[35,32,128]{2,1,0:T(8,128)S(1)} %get-tuple-element.20.edges, f32[3600,128]{1,0:T(8,128)S(1)} %get-tuple-element.21.inner), custom_call_target="tpu_custom_call" | custom-call | tf_op jit(solution)/shard_map/finish/pallas_call | solution.py:945
Async XLA Ops:
  5.7 18.9 %all-to-all-start = ((f32[32,1,2944]{2,1,0:T(1,128)}), f32[32,1,2944]{2,1,0:T(1,128)S(1)}, u32[]{:S(2)}, u32[]{:S(2)}) async-start(f32[32,1,2944]{2,1,0:T(1,128)} %get-tuple-element.14), calls=%async_computation | async-start | bytes 753664 | tf_op jit(solution)/shard_map/all_to_all | solution.py:917
where the time goes:
time: 39.9 us; the launch traced here: 39.6 us
  Pallas kernels  17 us (43%)
  blocking collectives  11.1 us (28%)
  starting transfers between devices  7.29 us (18%)
  waiting for transfers between devices  3.6 us (9%)
  between operations  0.66 us (2%)
    all_to_all x1, blocking collectives, on_device(): hands = lax.all_to_all(hand, BOTH, 0, 0, tiled=True)  11.1 us
    pallas_call x1, Pallas kernels, on_device(): pl.pallas_call(functools.partial(tracer_kernel, levels, per, 4 * count),...  7.97 us
    all_to_all x1, starting transfers between devices, on_device(): rims = lax.all_to_all(slots, BOTH, 0, 0, tiled=True)  7.29 us
    pallas_call x1, Pallas kernels, on_device(): pl.pallas_call(functools.partial(forcing_kernel, levels, few, nx, ny), in...  5.02 us
    all_to_all x1, waiting for transfers between devices, on_device(): rims = lax.all_to_all(slots, BOTH, 0, 0, tiled=True)  3.6 us
    pallas_call x1, Pallas kernels, on_device(): pl.pallas_call(functools.partial(solve_kernel, levels, ny), in_specs=[pl....  2.23 us
    pallas_call x1, Pallas kernels, on_device(): pl.pallas_call(functools.partial(finish_kernel, levels, per), in_specs=[h...  1.82 us
  transfers between devices with their start and end apart: 1, of which 1 were waited for; matrix products, arithmetic and copies ran while one was open for 0% of the time, Pallas kernels for 20%

commit v1 on v0

--- a/solution.py
+++ b/solution.py
@@ -64,7 +64,12 @@
             low, high = max(c * rows, j * count), min((c + 1) * rows, (j + 1) * count)
             if low < high:
                 runs[c].append((j, low - j * count, low - c * rows, high - low))
-    return number, runs
+    merged = count <= 2 * rows and levels <= 12
+    return number, runs, number + (0 if merged else 1), 0 if merged else 1
+
+
+def gram_lane(n):
+    return 16 * (n // 4) + 12 + n % 4
 
 
 class Level:
@@ -141,10 +146,11 @@
 
 
 def choose(planes, lane, get):
-    value = get(planes[0])
-    for j in range(1, GROUP):
-        low = (OFF[j] - (32 if planes is LAST else 0)) % LANES
-        value = jnp.where(jnp.logical_and(lane >= low, lane < low + 16), get(planes[j]), value)
+    shift = 32 if planes is LAST else 0
+    lows = sorted(((OFF[j] - shift) % LANES, planes[j]) for j in range(GROUP))
+    value = get(lows[-1][1])
+    for low, a in reversed(lows[:-1]):
+        value = jnp.where(lane < low + 16, get(a), value)
     return value
 
 
@@ -157,7 +163,7 @@
 ):
     count = pos.shape[0]
     steps = levels // per
-    number_pieces, runs = pieces_of(levels, count)
+    number_pieces, runs, _, _ = pieces_of(levels, count)
     slot = RIM_ROWS + number_pieces
     pairs = []
     for step in range(steps):
@@ -400,9 +406,8 @@
 ):
     copies = fetching([(around_in, around)], sem)
     count = rims.shape[0]
-    number_pieces, _ = pieces_of(levels, count)
+    number_pieces, _, share, first = pieces_of(levels, count)
     slot = RIM_ROWS + number_pieces
-    share = 1 + number_pieces
     came = rims.reshape(count * slot, LANES)
     hand = hands.reshape(count * share, LANES)
     own = fields.at[pl.ds(PACKS, 56)]
@@ -429,7 +434,7 @@
 
         def relay(d, carry, n=n, base=base):
             row = around[base + d] + n
-            hand[pl.ds(d * share + 1 + n, 1), :] = came[pl.ds(row, 1), :]
+            hand[pl.ds(d * share + first + n, 1), :] = came[pl.ds(row, 1), :]
             return carry
 
         for d in range(count):
@@ -598,9 +603,12 @@
             pair += 1
     rows[pair : pair + 1] = jnp.where(one == 0, top, 0.0)
     total = jnp.sum(rows[...], axis=1, keepdims=True)
-    spot = row_of((16, LANES)) == lane_of((16, LANES))
+    spot = lane_of((16, LANES)) == gram_lane(row_of((16, LANES)))
     line = jnp.sum(jnp.where(spot, total, 0.0), axis=0, keepdims=True)
-    hand[pl.ds(0, count, stride=share), :] = jnp.broadcast_to(line, (count, LANES))
+    line = jnp.broadcast_to(line, (count, LANES))
+    if first == 0:
+        line = jnp.where(lane_of((count, LANES)) % 16 < 12, hand[pl.ds(0, count, stride=share), :], line)
+    hand[pl.ds(0, count, stride=share), :] = line
 
 
 def finish_kernel(
@@ -608,8 +616,7 @@
     cells, flat, left, right, message, out_sems,
 ):
     count = hands.shape[0]
-    number_pieces, runs = pieces_of(levels, count)
-    share = 1 + number_pieces
+    _, runs, share, first = pieces_of(levels, count)
     came = hands.reshape(count * share, LANES)
     steps = levels // per
     chunks = [pl.ds(step * per * ROWS, per * ROWS) for step in range(steps)]
@@ -619,10 +626,10 @@
     pair = 0
     for k in range(5):
         for i in range(k + 1):
-            value = jnp.sum(jnp.where(one == pair, row, 0.0), axis=1, keepdims=True)
+            value = jnp.sum(jnp.where(one == gram_lane(pair), row, 0.0), axis=1, keepdims=True)
             entry[i, k] = entry[k, i] = value
             pair += 1
-    top = jnp.sum(jnp.where(one == pair, row, 0.0), axis=1, keepdims=True) * (1.0 / count)
+    top = jnp.sum(jnp.where(one == gram_lane(pair), row, 0.0), axis=1, keepdims=True) * (1.0 / count)
 
     def image(c):
         out = [None] * 5
@@ -690,7 +697,7 @@
 
     for c in range(4):
         for j, device, low, size in runs[c ^ 1]:
-            value = came[pl.ds(device * share + 1 + j, size, stride=share), :]
+            value = came[pl.ds(device * share + first + j, size, stride=share), :]
             message[c, low : low + size] = value
     second = lane_of((SLABS, LANES)) % 16 == 1
     sums = []
@@ -897,9 +904,8 @@
     plane = vmem(PLANES, GROUPS, LANES)
     tall = vmem(PLANES, 40, LANES)
     numbers = pltpu.SMEM((count,), jnp.int32)
-    number_pieces, _ = pieces_of(levels, count)
+    number_pieces, _, share, _ = pieces_of(levels, count)
     slot = RIM_ROWS + number_pieces
-    share = 1 + number_pieces
     fields, slots, around = pl.pallas_call(
         functools.partial(forcing_kernel, levels, few, nx, ny),
         in_specs=[hbm] * 8,

time: 39.9 us -> 39.8 us (level)
  no operation moved by 1% of the time
where the time goes in v1:
time: 39.8 us; the launch traced here: 39.5 us
  Pallas kernels  17 us (43%)
  blocking collectives  11 us (28%)
  starting transfers between devices  7.3 us (18%)
  waiting for transfers between devices  3.63 us (9%)
  between operations  0.66 us (2%)
    all_to_all x1, blocking collectives, on_device(): hands = lax.all_to_all(hand, BOTH, 0, 0, tiled=True)  11 us
    pallas_call x1, Pallas kernels, on_device(): pl.pallas_call(functools.partial(tracer_kernel, levels, per, 4 * count),...  7.95 us
    all_to_all x1, starting transfers between devices, on_device(): rims = lax.all_to_all(slots, BOTH, 0, 0, tiled=True)  7.3 us
    pallas_call x1, Pallas kernels, on_device(): pl.pallas_call(functools.partial(forcing_kernel, levels, few, nx, ny), in...  5.01 us
    all_to_all x1, waiting for transfers between devices, on_device(): rims = lax.all_to_all(slots, BOTH, 0, 0, tiled=True)  3.63 us
    pallas_call x1, Pallas kernels, on_device(): pl.pallas_call(functools.partial(solve_kernel, levels, ny), in_specs=[pl....  2.24 us
    pallas_call x1, Pallas kernels, on_device(): pl.pallas_call(functools.partial(finish_kernel, levels, per), in_specs=[h...  1.8 us
  transfers between devices with their start and end apart: 1, of which 1 were waited for; matrix products, arithmetic and copies ran while one was open for 0% of the time, Pallas kernels for 20%

profile of v1, /device:TPU:0, one launch (start us, length us, event | category | flops | bytes accessed | tf_op | source)
XLA Modules:
  0.0 39.5 jit_solution(4225841634864330624)
XLA Ops:
  0.6 5.0 %forcing.1 = (f32[968,128]{1,0:T(8,128)S(1)}, f32[32,1,2944]{2,1,0:T(1,128)}, s32[136]{0:T(256)S(1)}) custom-call(s32[32]{0:T(128)} %pos_in.1, f32[3600,128]{1,0:T(8,128)} %bitcast.5, f32[3600,128]{1,0:T(8,128)} %bitcast.7, f32[3600,128]{1,0:T(8,128)} %bitcast.9, f32[1,38400]{1,0:T(1,128)} %depth_in.1, s32[1,38400]{1,0:T(1,128)} %ocean_in.1, ...), custom_call_target="tpu_custom_call" | custom-call | tf_op jit(solution)/shard_map/forcing/pallas_call | solution.py:909
  5.6 7.3 %all-to-all-start = ((f32[32,1,2944]{2,1,0:T(1,128)}), f32[32,1,2944]{2,1,0:T(1,128)S(1)}, u32[]{:S(2)}, u32[]{:S(2)}) async-start(f32[32,1,2944]{2,1,0:T(1,128)} %get-tuple-element.14), calls=%async_computation | async-start | bytes 753664 | tf_op jit(solution)/shard_map/all_to_all | solution.py:923
  13.0 7.9 %tracer.1 = (f32[3600,128]{1,0:T(8,128)S(1)}, f32[35,32,128]{2,1,0:T(8,128)S(1)}) custom-call(s32[136]{0:T(256)S(1)} %get-tuple-element.13.around.around_in, f32[3600,128]{1,0:T(8,128)} %bitcast.6, f32[3600,128]{1,0:T(8,128)} %bitcast.8, f32[3600,128]{1,0:T(8,128)} %bitcast.10, f32[11,1,38400]{2,1,0:T(1,128)} %bitcast.11, ...), custom_call_target="tpu_custom_call" | custom-call | tf_op jit(solution)/shard_map/tracer/pallas_call | solution.py:925
  20.9 3.6 %all-to-all-done.rims = f32[32,1,2944]{2,1,0:T(1,128)S(1)} async-done(((f32[32,1,2944]{2,1,0:T(1,128)}), f32[32,1,2944]{2,1,0:T(1,128)S(1)}, u32[]{:S(2)}, u32[]{:S(2)}) %all-to-all-start) | async-done | bytes 376864 | tf_op jit(solution)/shard_map/all_to_all | solution.py:923
  24.5 2.2 %vectors.1 = (f32[4,8,24,256]{3,2,1,0:T(8,128)S(1)}, f32[32,1,384]{2,1,0:T(1,128)S(1)}) custom-call(s32[136]{0:T(256)S(1)} %get-tuple-element.13.around.around_in, f32[32,1,2944]{2,1,0:T(1,128)S(1)} %all-to-all-done.rims, f32[968,128]{1,0:T(8,128)S(1)} %get-tuple-element.15.fields), custom_call_target="tpu_custom_call" | custom-call | tf_op jit(solution)/shard_map/vectors/pallas_call | solution.py:939
  26.8 11.0 %all_to_all.10.hands = f32[32,1,384]{2,1,0:T(1,128)S(1)} all-to-all(f32[32,1,384]{2,1,0:T(1,128)S(1)} %get-tuple-element.18), channel_id=1, replica_groups=mesh['gx'=8,'gy'=4] {'gx','gy'}, dimensions={0} | all-to-all | bytes 98304 | tf_op jit(solution)/shard_map/all_to_all | solution.py:949
  37.7 1.8 %finish.1 = (f32[3600,128]{1,0:T(8,128)}, f32[1,38400]{1,0:T(1,128)}) custom-call(f32[32,1,384]{2,1,0:T(1,128)S(1)} %all_to_all.10.hands, f32[4,8,24,256]{3,2,1,0:T(8,128)S(1)} %get-tuple-element.19.vectors, f32[35,32,128]{2,1,0:T(8,128)S(1)} %get-tuple-element.20.edges, f32[3600,128]{1,0:T(8,128)S(1)} %get-tuple-element.21.inner), custom_call_target="tpu_custom_call" | custom-call | tf_op jit(solution)/shard_map/finish/pallas_call | solution.py:951
Async XLA Ops:
  5.6 18.9 %all-to-all-start = ((f32[32,1,2944]{2,1,0:T(1,128)}), f32[32,1,2944]{2,1,0:T(1,128)S(1)}, u32[]{:S(2)}, u32[]{:S(2)}) async-start(f32[32,1,2944]{2,1,0:T(1,128)} %get-tuple-element.14), calls=%async_computation | async-start | bytes 753664 | tf_op jit(solution)/shard_map/all_to_all | solution.py:923

commit v2 on v1

--- a/solution.py
+++ b/solution.py
@@ -76,8 +76,8 @@
     def __init__(self, ref, base):
         self.ref, self.base = ref, base
 
-    def plane(self, a):
-        return self.ref[comb(self.base + a), :]
+    def plane(self, a, low=0, size=GROUPS):
+        return self.ref[comb(self.base + a, size, low), :]
 
     def rows(self, low, size):
         return self.ref[pl.ds(self.base + low, size), :]
@@ -91,8 +91,8 @@
     return lax.broadcasted_iota(jnp.int32, shape, 0)
 
 
-def comb(a, count=GROUPS):
-    return pl.ds(a, count, stride=PLANES)
+def comb(a, count=GROUPS, low=0):
+    return pl.ds(low * PLANES + a, count, stride=PLANES)
 
 
 def line_of(get, y):
@@ -112,12 +112,12 @@
     return value
 
 
-def store_terms(a, temp, flow_x, flow_y, te, tw, tn, ts):
+def store_terms(a, temp, flow_x, flow_y, te, tw, tn, ts, low=0, size=GROUPS):
     spread = DIFFUSE * temp
-    te[a] = spread - flow_x
-    tw[a] = spread + flow_x
-    tn[a, 8 : 8 + GROUPS] = spread - flow_y
-    ts[a, 8 : 8 + GROUPS] = spread + flow_y
+    te[a, low : low + size] = spread - flow_x
+    tw[a, low : low + size] = spread + flow_x
+    tn[a, 8 + low : 8 + low + size] = spread - flow_y
+    ts[a, 8 + low : 8 + low + size] = spread + flow_y
 
 
 def clear_terms(tn, ts):
@@ -127,18 +127,19 @@
         ref[:, 8 + GROUPS : 9 + GROUPS] = none
 
 
-def inner_sum(a, te, tw, tn, ts):
-    lane = lane_of((GROUPS, LANES))
-    here = te[a]
-    east = here if a == PLANES - 1 else jnp.where(lane == 0, te[a + 1], here)
+def inner_sum(a, te, tw, tn, ts, low=0, size=GROUPS):
+    lane = lane_of((size, LANES))
+    rows = slice(low, low + size)
+    here = te[a, rows]
+    east = here if a == PLANES - 1 else jnp.where(lane == 0, te[a + 1, rows], here)
     east = drop(turn(east, -1), LAST_OF[a], lane)
-    here = tw[a]
-    west = here if a == 0 else jnp.where(lane == LANES - 1, tw[a - 1], here)
+    here = tw[a, rows]
+    west = here if a == 0 else jnp.where(lane == LANES - 1, tw[a - 1, rows], here)
     west = drop(turn(west, 1), FIRST_OF[a], lane)
 
     def plane(ref, at):
-        down = 8 + (at >= PLANES) - (at < 0)
-        return ref[at % PLANES, down : down + GROUPS]
+        down = 8 + low + (at >= PLANES) - (at < 0)
+        return ref[at % PLANES, down : down + size]
 
     north = turn(jnp.where(lane >= LANES - 16, plane(tn, a + 1), plane(tn, a + 2)), 16)
     south = turn(jnp.where(lane < 16, plane(ts, a - 1), plane(ts, a - 2)), -16)
@@ -155,30 +156,33 @@
 
 
 def forcing_kernel(
-    levels, per, tiles_x, tiles_y,
+    levels, tiles_x, tiles_y,
     pos_in, temp_in, zonal_in, merid_in, depth_in, ocean_in, diag_in, source_in,
     fields, slots_out, around,
-    temp, zonal, merid, depth, ocean, source, slots,
+    temp_at, zonal_at, merid_at, depth, ocean, source, slots,
     st, sx, sy, pt, te, tw, tn, ts, edges, pos, holder, sems, out_sems,
 ):
     count = pos.shape[0]
-    steps = levels // per
     number_pieces, runs, _, _ = pieces_of(levels, count)
     slot = RIM_ROWS + number_pieces
-    pairs = []
-    for step in range(steps):
-        chunk = pl.ds(step * per * ROWS, per * ROWS)
+    blocks = [(low, min(8, GROUPS - low)) for low in range(0, GROUPS, 8)]
+    pairs = [(pos_in, pos)]
+    for n, (low, size) in enumerate(blocks):
+        cells = pl.ds(low * PLANES * LANES, size * PLANES * LANES)
         pairs += [
-            (a.at[chunk], b.at[chunk]) for a, b in ((temp_in, temp), (zonal_in, zonal), (merid_in, merid))
+            (a.at[:, :, cells], b.at[:, :, cells])
+            for a, b in ((temp_in, temp_at), (zonal_in, zonal_at), (merid_in, merid_at))
         ]
-    pairs += [
-        (a.reshape(ROWS, LANES), b)
-        for a, b in (
-            (source_in, source), (ocean_in, ocean), (depth_in, depth),
-            (diag_in, fields.at[pl.ds(2 * HELD, ROWS)]),
-        )
-    ]
-    copies = fetching([(pos_in, pos)] + pairs, sems)
+        if n == 0:
+            pairs += [
+                (a.reshape(ROWS, LANES), b)
+                for a, b in (
+                    (source_in, source), (ocean_in, ocean), (depth_in, depth),
+                    (diag_in, fields.at[pl.ds(2 * HELD, ROWS)]),
+                )
+            ]
+    copies = fetching(pairs, sems)
+    temp, zonal, merid = (ref.reshape(levels * ROWS, LANES) for ref in (temp_at, zonal_at, merid_at))
     copies.pop(0).wait()
     results = []
 
@@ -222,65 +226,10 @@
     lax.fori_loop(0, tiles_y, look, 0)
     clear_terms(tn, ts)
 
-    def add(flats, low, size, fresh):
-        rows = pl.ds(low, size)
-        total = [None] * 3
-        for t, u, v in zip(*flats):
-            t = t.rows(low, size)
-            new = (t, t * u.rows(low, size), t * v.rows(low, size))
-            total = [b if a is None else a + b for a, b in zip(total, new)]
-        for ref, value in zip((st, sx, sy), total):
-            ref[rows, :] = value if fresh else ref[rows, :] + value
-
-    for step in range(steps):
-        for copy in copies[3 * step : 3 * step + 3]:
-            copy.wait()
-        flats = [
-            [Level(ref, (step * per + n) * ROWS) for n in range(per)] for ref in (temp, zonal, merid)
-        ]
-
-        def some(m, carry):
-            add(flats, pl.multiple_of(m * 8, 8), 8, step == 0)
-            return carry
-
-        lax.fori_loop(0, ROWS // 8, some, 0, unroll=4)
-        if ROWS % 8:
-            add(flats, ROWS - ROWS % 8, ROWS % 8, step == 0)
-
-        for n in range(per):
-            k = step * per + n
-            t, u, v = (flat[n] for flat in flats)
-
-            loaded = {a: (t.plane(a), u.plane(a)) for a in sorted(set(START + LAST))}
-
-            def term(planes, sign):
-                own = choose(planes, lane, lambda a: loaded[a][0])
-                flow = choose(planes, lane, lambda a: loaded[a][1])
-                return DIFFUSE * own + sign * ADVECT * (flow * own)
-
-            edges[0, 0:GROUPS] = jnp.where(q == k, turn(term(START, -1.0), k), edges[0, 0:GROUPS])
-            edges[1, 0:GROUPS] = jnp.where(q == k, turn(term(LAST, 1.0), k + 17), edges[1, 0:GROUPS])
-            rows = t.rows(0, 2)
-            rows = DIFFUSE * rows - ADVECT * (v.rows(0, 2) * rows)
-            edges[2, k : k + 1] = rows[0:1]
-            edges[2, k + levels : k + levels + 1] = rows[1:2]
-            rows = t.rows(ROWS - 2, 2)
-            rows = DIFFUSE * rows + ADVECT * (v.rows(ROWS - 2, 2) * rows)
-            edges[3, k : k + 1] = turn(jnp.where(one >= 16, rows[0:1], rows[1:2]), -16)
-            edges[3, k + levels : k + levels + 1] = turn(rows[1:2], -16)
-
-    for c in range(4):
-        for j, device, low, size in runs[c]:
-            slots[pl.ds(device * slot + RIM_ROWS + j, size, stride=slot), :] = edges[c, low : low + size]
-
-    for copy in copies[3 * steps :]:
-        copy.wait()
-
     part = fields.at[pl.ds(0, HELD)]
     mask = fields.at[pl.ds(HELD, HELD)]
     diag = fields.at[pl.ds(2 * HELD, HELD)]
     own = fields.at[pl.ds(PACKS, 56)]
-    mask[0:ROWS] = depth[...] * ocean[...].astype(jnp.float32)
 
     def wet_of(rows):
         return ocean[rows, :].astype(jnp.float32)
@@ -288,15 +237,81 @@
     def masked(rows):
         return mask[rows, :]
 
-    for a in range(PLANES):
-        total = st[comb(a), :]
-        pt[a] = total
-        store_terms(a, total, ADVECT * sx[comb(a), :], ADVECT * sy[comb(a), :], te, tw, tn, ts)
-    for a in range(PLANES):
-        total = pt[a]
-        wet = wet_of(comb(a))
-        change = inner_sum(a, te, tw, tn, ts) - 4.0 * DIFFUSE * total
-        part[comb(a), :] = source[comb(a), :] + (STERIC / levels) * wet * (total + wet * change)
+    def add(low, size):
+        total = [None] * 3
+        for k in range(levels):
+            rows = pl.ds(k * ROWS + low, size)
+            t = temp[rows, :]
+            new = (t, t * zonal[rows, :], t * merid[rows, :])
+            total = [b if a is None else a + b for a, b in zip(total, new)]
+        for ref, value in zip((st, sx, sy), total):
+            ref[pl.ds(low, size), :] = value
+
+    def finish_part(low, size):
+        for a in range(PLANES):
+            rows = comb(a, size, low)
+            total = pt[a, low : low + size]
+            wet = wet_of(rows)
+            change = inner_sum(a, te, tw, tn, ts, low, size) - 4.0 * DIFFUSE * total
+            part[rows, :] = source[rows, :] + (STERIC / levels) * wet * (total + wet * change)
+
+    for n, (low, size) in enumerate(blocks):
+        for copy in copies[:3]:
+            copy.wait()
+        del copies[:3]
+
+        def some(m, carry, low=low):
+            add(low * PLANES + m * 8, 8)
+            return carry
+
+        lax.fori_loop(0, size * PLANES // 8, some, 0)
+        if size * PLANES % 8:
+            rest = size * PLANES % 8
+            add((low + size) * PLANES - rest, rest)
+        for a in range(PLANES):
+            rows = comb(a, size, low)
+            total = st[rows, :]
+            pt[a, low : low + size] = total
+            store_terms(
+                a, total, ADVECT * sx[rows, :], ADVECT * sy[rows, :], te, tw, tn, ts, low, size
+            )
+
+        some_lanes = lane_of((size, LANES))
+        some_q = some_lanes % 16
+        for c, planes, sign, more in ((0, START, -1.0, 0), (1, LAST, 1.0, 17)):
+            pack = jnp.zeros((size, LANES), jnp.float32)
+            for k in range(levels):
+                t, u = Level(temp, k * ROWS), Level(zonal, k * ROWS)
+                value = choose(planes, some_lanes, lambda a: t.plane(a, low, size))
+                flow = choose(planes, some_lanes, lambda a: u.plane(a, low, size))
+                value = DIFFUSE * value + sign * ADVECT * (flow * value)
+                pack = jnp.where(some_q == k, turn(value, k + more), pack)
+            edges[c, low : low + size] = pack
+        for c, at, sign in ((2, 0, -1.0), (3, ROWS - 2, 1.0)):
+            if n != (0 if c == 2 else len(blocks) - 1):
+                continue
+            for k in range(levels):
+                rows = pl.ds(k * ROWS + at, 2)
+                value = temp[rows, :]
+                value = DIFFUSE * value + sign * ADVECT * (merid[rows, :] * value)
+                left, right = value[0:1], value[1:2]
+                if c == 3:
+                    left, right = turn(jnp.where(one >= 16, left, right), -16), turn(right, -16)
+                edges[c, k : k + 1] = left
+                edges[c, k + levels : k + levels + 1] = right
+
+        if n == 0:
+            for copy in copies[:4]:
+                copy.wait()
+            del copies[:4]
+            mask[0:ROWS] = depth[...] * ocean[...].astype(jnp.float32)
+        else:
+            finish_part(*blocks[n - 1])
+
+    for c in range(4):
+        for j, device, low, size in runs[c]:
+            slots[pl.ds(device * slot + RIM_ROWS + j, size, stride=slot), :] = edges[c, low : low + size]
+    finish_part(*blocks[-1])
 
     def mix(*values):
         value = values[-1]
@@ -875,13 +890,16 @@
     f32 = jnp.float32
     per = next(n for n in (4, 2, 6, levels) if levels % n == 0 and n * ROWS % 8 == 0)
     steps = levels // per
-    few = next(n for n in (2, 4, 6, levels) if levels % n == 0 and n * ROWS % 8 == 0)
     params = pltpu.CompilerParams(vmem_limit_bytes=BUDGET)
     temp, zonal, merid = (
         array.reshape(levels * ROWS, LANES)
         for array in (thermal_anomaly, zonal_flow_ratio, meridional_flow_ratio)
     )
     rates = diffusion_rates.reshape(levels - 1, 1, cells)
+    by_cells = [
+        pltpu.with_memory_space_constraint(array.reshape(levels, 1, cells), pltpu.HBM)
+        for array in (temp, zonal, merid)
+    ]
     temp, zonal, merid, rates, depth, ocean, diag, source, positions = (
         pltpu.with_memory_space_constraint(array, pltpu.HBM)
         for array in (temp, zonal, merid, rates, depth, ocean, diag, source, block_positions)
@@ -907,19 +925,19 @@
     number_pieces, _, share, _ = pieces_of(levels, count)
     slot = RIM_ROWS + number_pieces
     fields, slots, around = pl.pallas_call(
-        functools.partial(forcing_kernel, levels, few, nx, ny),
+        functools.partial(forcing_kernel, levels, nx, ny),
         in_specs=[hbm] * 8,
         out_specs=[here, hbm, SMEM],
         out_shape=[
             out(FIELDS, LANES), pltpu.HBM((count, 1, slot * LANES), f32), out(4 * count + 8, kind=jnp.int32),
         ],
-        scratch_shapes=[deep] * 3 + [flat, flat_int, flat]
+        scratch_shapes=[vmem(levels, 1, cells)] * 3 + [flat, flat_int, flat]
         + [vmem(count * slot, LANES)]
         + [flat] * 3 + [plane] * 3 + [tall] * 2
-        + [vmem(4, 2 * levels, LANES), numbers, numbers, sems(3 * (levels // few) + 5), sems(1)],
+        + [vmem(4, 2 * levels, LANES), numbers, numbers, sems(3 * len(range(0, GROUPS, 8)) + 5), sems(1)],
         compiler_params=params,
         name="forcing",
-    )(positions, temp, zonal, merid, depth, ocean, diag, source)
+    )(positions, *by_cells, depth, ocean, diag, source)
     rims = lax.all_to_all(slots, BOTH, 0, 0, tiled=True)
 
     inner, edges = pl.pallas_call(

time: 39.8 us -> 40 us (level)
  no operation moved by 1% of the time
where the time goes in v2:
time: 40 us; the launch traced here: 39.8 us
  Pallas kernels  17.3 us (43%)
  blocking collectives  11 us (28%)
  starting transfers between devices  7.3 us (18%)
  waiting for transfers between devices  3.63 us (9%)
  between operations  0.66 us (2%)
    all_to_all x1, blocking collectives, on_device(): hands = lax.all_to_all(hand, BOTH, 0, 0, tiled=True)  11 us
    pallas_call x1, Pallas kernels, on_device(): pl.pallas_call(functools.partial(tracer_kernel, levels, per, 4 * count),...  7.95 us
    all_to_all x1, starting transfers between devices, on_device(): rims = lax.all_to_all(slots, BOTH, 0, 0, tiled=True)  7.3 us
    pallas_call x1, Pallas kernels, on_device(): pl.pallas_call(functools.partial(forcing_kernel, levels, nx, ny), in_spec...  5.27 us
    all_to_all x1, waiting for transfers between devices, on_device(): rims = lax.all_to_all(slots, BOTH, 0, 0, tiled=True)  3.63 us
    pallas_call x1, Pallas kernels, on_device(): pl.pallas_call(functools.partial(solve_kernel, levels, ny), in_specs=[pl....  2.24 us
    pallas_call x1, Pallas kernels, on_device(): pl.pallas_call(functools.partial(finish_kernel, levels, per), in_specs=[h...  1.8 us
  transfers between devices with their start and end apart: 1, of which 1 were waited for; matrix products, arithmetic and copies ran while one was open for 0% of the time, Pallas kernels for 20%

profile of v2, /device:TPU:0, one launch (start us, length us, event | category | flops | bytes accessed | tf_op | source)
XLA Modules:
  0.0 39.8 jit_solution(9209009791416208009)
XLA Ops:
  0.6 5.3 %forcing.1 = (f32[968,128]{1,0:T(8,128)S(1)}, f32[32,1,2944]{2,1,0:T(1,128)}, s32[136]{0:T(256)S(1)}) custom-call(s32[32]{0:T(128)} %pos_in.1, f32[12,1,38400]{2,1,0:T(1,128)} %bitcast.8, f32[12,1,38400]{2,1,0:T(1,128)} %bitcast.10, f32[12,1,38400]{2,1,0:T(1,128)} %bitcast.12, f32[1,38400]{1,0:T(1,128)} %depth_in.1, s32[1,38400]{1,0:T(1,128)} %ocean_in.1, ...), custom_call_target="tpu_custom_call" | custom-call | tf_op jit(solution)/shard_map/forcing/pallas_call | solution.py:927
  5.9 7.3 %all-to-all-start = ((f32[32,1,2944]{2,1,0:T(1,128)}), f32[32,1,2944]{2,1,0:T(1,128)S(1)}, u32[]{:S(2)}, u32[]{:S(2)}) async-start(f32[32,1,2944]{2,1,0:T(1,128)} %get-tuple-element.14), calls=%async_computation | async-start | bytes 753664 | tf_op jit(solution)/shard_map/all_to_all | solution.py:941
  13.2 7.9 %tracer.1 = (f32[3600,128]{1,0:T(8,128)S(1)}, f32[35,32,128]{2,1,0:T(8,128)S(1)}) custom-call(s32[136]{0:T(256)S(1)} %get-tuple-element.13.around.around_in, f32[3600,128]{1,0:T(8,128)} %bitcast.9, f32[3600,128]{1,0:T(8,128)} %bitcast.11, f32[3600,128]{1,0:T(8,128)} %bitcast.13, f32[11,1,38400]{2,1,0:T(1,128)} %bitcast.14, ...), custom_call_target="tpu_custom_call" | custom-call | tf_op jit(solution)/shard_map/tracer/pallas_call | solution.py:943
  21.2 3.6 %all-to-all-done.rims = f32[32,1,2944]{2,1,0:T(1,128)S(1)} async-done(((f32[32,1,2944]{2,1,0:T(1,128)}), f32[32,1,2944]{2,1,0:T(1,128)S(1)}, u32[]{:S(2)}, u32[]{:S(2)}) %all-to-all-start) | async-done | bytes 376864 | tf_op jit(solution)/shard_map/all_to_all | solution.py:941
  24.8 2.2 %vectors.1 = (f32[4,8,24,256]{3,2,1,0:T(8,128)S(1)}, f32[32,1,384]{2,1,0:T(1,128)S(1)}) custom-call(s32[136]{0:T(256)S(1)} %get-tuple-element.13.around.around_in, f32[32,1,2944]{2,1,0:T(1,128)S(1)} %all-to-all-done.rims, f32[968,128]{1,0:T(8,128)S(1)} %get-tuple-element.15.fields), custom_call_target="tpu_custom_call" | custom-call | tf_op jit(solution)/shard_map/vectors/pallas_call | solution.py:957
  27.0 11.0 %all_to_all.10.hands = f32[32,1,384]{2,1,0:T(1,128)S(1)} all-to-all(f32[32,1,384]{2,1,0:T(1,128)S(1)} %get-tuple-element.18), channel_id=1, replica_groups=mesh['gx'=8,'gy'=4] {'gx','gy'}, dimensions={0} | all-to-all | bytes 98304 | tf_op jit(solution)/shard_map/all_to_all | solution.py:967
  38.0 1.8 %finish.1 = (f32[3600,128]{1,0:T(8,128)}, f32[1,38400]{1,0:T(1,128)}) custom-call(f32[32,1,384]{2,1,0:T(1,128)S(1)} %all_to_all.10.hands, f32[4,8,24,256]{3,2,1,0:T(8,128)S(1)} %get-tuple-element.19.vectors, f32[35,32,128]{2,1,0:T(8,128)S(1)} %get-tuple-element.20.edges, f32[3600,128]{1,0:T(8,128)S(1)} %get-tuple-element.21.inner), custom_call_target="tpu_custom_call" | custom-call | tf_op jit(solution)/shard_map/finish/pallas_call | solution.py:969
Async XLA Ops:
  5.9 18.9 %all-to-all-start = ((f32[32,1,2944]{2,1,0:T(1,128)}), f32[32,1,2944]{2,1,0:T(1,128)S(1)}, u32[]{:S(2)}, u32[]{:S(2)}) async-start(f32[32,1,2944]{2,1,0:T(1,128)} %get-tuple-element.14), calls=%async_computation | async-start | bytes 753664 | tf_op jit(solution)/shard_map/all_to_all | solution.py:941

commit v3 on v1

--- a/solution.py
+++ b/solution.py
@@ -157,9 +157,9 @@
 def forcing_kernel(
     levels, per, tiles_x, tiles_y,
     pos_in, temp_in, zonal_in, merid_in, depth_in, ocean_in, diag_in, source_in,
-    fields, slots_out, around,
+    fields, slots_out, around_out,
     temp, zonal, merid, depth, ocean, source, slots,
-    st, sx, sy, pt, te, tw, tn, ts, edges, pos, holder, sems, out_sems,
+    st, sx, sy, pt, te, tw, tn, ts, edges, pos, holder, around, sems, out_sems,
 ):
     count = pos.shape[0]
     steps = levels // per
@@ -220,6 +220,7 @@
         return carry
 
     lax.fori_loop(0, tiles_y, look, 0)
+    send(around, around_out)
     clear_terms(tn, ts)
 
     def add(flats, low, size, fresh):
@@ -909,14 +910,15 @@
     fields, slots, around = pl.pallas_call(
         functools.partial(forcing_kernel, levels, few, nx, ny),
         in_specs=[hbm] * 8,
-        out_specs=[here, hbm, SMEM],
+        out_specs=[here, hbm, hbm],
         out_shape=[
             out(FIELDS, LANES), pltpu.HBM((count, 1, slot * LANES), f32), out(4 * count + 8, kind=jnp.int32),
         ],
         scratch_shapes=[deep] * 3 + [flat, flat_int, flat]
         + [vmem(count * slot, LANES)]
         + [flat] * 3 + [plane] * 3 + [tall] * 2
-        + [vmem(4, 2 * levels, LANES), numbers, numbers, sems(3 * (levels // few) + 5), sems(1)],
+        + [vmem(4, 2 * levels, LANES), numbers, numbers]
+        + [pltpu.SMEM((4 * count + 8,), jnp.int32), sems(3 * (levels // few) + 5), sems(2)],
         compiler_params=params,
         name="forcing",
     )(positions, temp, zonal, merid, depth, ocean, diag, source)

time: 39.8 us -> 39.2 us (0.985)
  Pallas kernels: 17 us -> 16.4 us
    pallas_call x1, Pallas kernels: 5.01 us -> 4.42 us  [on_device(): pl.pallas_call(functools.partial(forcing_kernel, levels, few, nx, ny), in...]
where the time goes in v3:
time: 39.2 us; the launch traced here: 38.9 us
  Pallas kernels  16.4 us (42%)
  blocking collectives  11 us (28%)
  starting transfers between devices  7.29 us (19%)
  waiting for transfers between devices  3.63 us (9%)
  between operations  0.66 us (2%)
    all_to_all x1, blocking collectives, on_device(): hands = lax.all_to_all(hand, BOTH, 0, 0, tiled=True)  11 us
    pallas_call x1, Pallas kernels, on_device(): pl.pallas_call(functools.partial(tracer_kernel, levels, per, 4 * count),...  7.95 us
    all_to_all x1, starting transfers between devices, on_device(): rims = lax.all_to_all(slots, BOTH, 0, 0, tiled=True)  7.29 us
    pallas_call x1, Pallas kernels, on_device(): pl.pallas_call(functools.partial(forcing_kernel, levels, few, nx, ny), in...  4.42 us
    all_to_all x1, waiting for transfers between devices, on_device(): rims = lax.all_to_all(slots, BOTH, 0, 0, tiled=True)  3.63 us
    pallas_call x1, Pallas kernels, on_device(): pl.pallas_call(functools.partial(solve_kernel, levels, ny), in_specs=[pl....  2.24 us
    pallas_call x1, Pallas kernels, on_device(): pl.pallas_call(functools.partial(finish_kernel, levels, per), in_specs=[h...  1.8 us
  transfers between devices with their start and end apart: 1, of which 1 were waited for; matrix products, arithmetic and copies ran while one was open for 0% of the time, Pallas kernels for 20%

profile of v3, /device:TPU:0, one launch (start us, length us, event | category | flops | bytes accessed | tf_op | source)
XLA Modules:
  0.0 38.9 jit_solution(8209256173904177742)
XLA Ops:
  0.6 4.4 %forcing.1 = (f32[968,128]{1,0:T(8,128)S(1)}, f32[32,1,2944]{2,1,0:T(1,128)}, s32[136]{0:T(256)S(1)}) custom-call(s32[32]{0:T(128)} %pos_in.1, f32[3600,128]{1,0:T(8,128)} %bitcast.5, f32[3600,128]{1,0:T(8,128)} %bitcast.7, f32[3600,128]{1,0:T(8,128)} %bitcast.9, f32[1,38400]{1,0:T(1,128)} %depth_in.1, s32[1,38400]{1,0:T(1,128)} %ocean_in.1, ...), custom_call_target="tpu_custom_call" | custom-call | tf_op jit(solution)/shard_map/forcing/pallas_call | solution.py:910
  5.1 7.3 %all-to-all-start = ((f32[32,1,2944]{2,1,0:T(1,128)}), f32[32,1,2944]{2,1,0:T(1,128)S(1)}, u32[]{:S(2)}, u32[]{:S(2)}) async-start(f32[32,1,2944]{2,1,0:T(1,128)} %get-tuple-element.14), calls=%async_computation | async-start | bytes 753664 | tf_op jit(solution)/shard_map/all_to_all | solution.py:925
  12.3 7.9 %tracer.1 = (f32[3600,128]{1,0:T(8,128)S(1)}, f32[35,32,128]{2,1,0:T(8,128)S(1)}) custom-call(s32[136]{0:T(256)S(1)} %get-tuple-element.13.around.around_in, f32[3600,128]{1,0:T(8,128)} %bitcast.6, f32[3600,128]{1,0:T(8,128)} %bitcast.8, f32[3600,128]{1,0:T(8,128)} %bitcast.10, f32[11,1,38400]{2,1,0:T(1,128)} %bitcast.11, ...), custom_call_target="tpu_custom_call" | custom-call | tf_op jit(solution)/shard_map/tracer/pallas_call | solution.py:927
  20.3 3.6 %all-to-all-done.rims = f32[32,1,2944]{2,1,0:T(1,128)S(1)} async-done(((f32[32,1,2944]{2,1,0:T(1,128)}), f32[32,1,2944]{2,1,0:T(1,128)S(1)}, u32[]{:S(2)}, u32[]{:S(2)}) %all-to-all-start) | async-done | bytes 376864 | tf_op jit(solution)/shard_map/all_to_all | solution.py:925
  23.9 2.2 %vectors.1 = (f32[4,8,24,256]{3,2,1,0:T(8,128)S(1)}, f32[32,1,384]{2,1,0:T(1,128)S(1)}) custom-call(s32[136]{0:T(256)S(1)} %get-tuple-element.13.around.around_in, f32[32,1,2944]{2,1,0:T(1,128)S(1)} %all-to-all-done.rims, f32[968,128]{1,0:T(8,128)S(1)} %get-tuple-element.15.fields), custom_call_target="tpu_custom_call" | custom-call | tf_op jit(solution)/shard_map/vectors/pallas_call | solution.py:941
  26.2 11.0 %all_to_all.10.hands = f32[32,1,384]{2,1,0:T(1,128)S(1)} all-to-all(f32[32,1,384]{2,1,0:T(1,128)S(1)} %get-tuple-element.18), channel_id=1, replica_groups=mesh['gx'=8,'gy'=4] {'gx','gy'}, dimensions={0} | all-to-all | bytes 98304 | tf_op jit(solution)/shard_map/all_to_all | solution.py:951
  37.1 1.8 %finish.1 = (f32[3600,128]{1,0:T(8,128)}, f32[1,38400]{1,0:T(1,128)}) custom-call(f32[32,1,384]{2,1,0:T(1,128)S(1)} %all_to_all.10.hands, f32[4,8,24,256]{3,2,1,0:T(8,128)S(1)} %get-tuple-element.19.vectors, f32[35,32,128]{2,1,0:T(8,128)S(1)} %get-tuple-element.20.edges, f32[3600,128]{1,0:T(8,128)S(1)} %get-tuple-element.21.inner), custom_call_target="tpu_custom_call" | custom-call | tf_op jit(solution)/shard_map/finish/pallas_call | solution.py:953
Async XLA Ops:
  5.1 18.9 %all-to-all-start = ((f32[32,1,2944]{2,1,0:T(1,128)}), f32[32,1,2944]{2,1,0:T(1,128)S(1)}, u32[]{:S(2)}, u32[]{:S(2)}) async-start(f32[32,1,2944]{2,1,0:T(1,128)} %get-tuple-element.14), calls=%async_computation | async-start | bytes 753664 | tf_op jit(solution)/shard_map/all_to_all | solution.py:925
